TPU v7x, 128 devices: a whole 4x4x4 slice. The times are simulated.
128 devices in a mesh: dp: 8 (over z, core), tensor: 16 (over y, x).
Axes of the slice: x: 4, y: 4, z: 4, core: 2. Of those that a mesh axis runs over, the one named last changes fastest.
Arguments:
- activations: bfloat16 [65536, 4096], P(('dp', 'tensor')), may hold values from -6 to 6
- cotangent: bfloat16 [65536, 11008], P('dp', 'tensor'), may hold values from -0.008178711 to 0.008178711
- projection: bfloat16 [4096, 512], replicated, may hold values from -0.25 to 0.25
- first_moment: float32 [512, 11008], P('dp', 'tensor'), may hold values from -0.6 to 0.6
- second_moment: float32 [512, 11008], P('dp', 'tensor'), may hold values from 0.01 to 1
- step_count: int32 [1], replicated, may hold values from 1 to 39
Outputs:
- update: bfloat16 [4096, 11008], P('dp', 'tensor')
- new_first: float32 [512, 11008], P('dp', 'tensor')
- new_second: float32 [512, 11008], P('dp', 'tensor')
All inputs are finite; a program needn't handle non-finite values.
Results may differ from a plain program's by a relative error of at most 0.0055.
Values may be sent and summed in bfloat16 or wider, within the bound.
A program may use at most 128 MiB of HBM per device.

v0:
```python
import jax
import jax.numpy as jnp
from jax import lax
from jax.sharding import PartitionSpec as P


def in_blocks(shard, dim, count):
    before, after = (shard.shape[:dim], shard.shape[dim + 1 :])
    return jnp.moveaxis(shard.reshape(*before, count, -1, *after), dim, 0)


def sum_at_owner(shard, axis, dim):
    count = lax.axis_size(axis)
    parts = lax.all_to_all(in_blocks(shard, dim, count), axis, 0, 0, tiled=True)
    return jnp.sum(parts, axis=0)


def laid_out(parts, dim):
    parts = jnp.moveaxis(parts, 0, dim)
    shape = parts.shape
    return parts.reshape(*shape[:dim], shape[dim] * shape[dim + 1], *shape[dim + 2 :])


def sent_to_all(shard, axis):
    count = lax.axis_size(axis)
    return lax.all_to_all(
        jnp.broadcast_to(shard[None], (count, *shard.shape)), axis, 0, 0, tiled=True
    )


def gather_directly(shard, axis, dim):
    return laid_out(sent_to_all(shard, axis), dim)


def per_device(activations, cotangent, projection, first_moment, second_moment, step_count):
    projected = jnp.dot(activations, projection, preferred_element_type=jnp.float32).astype(
        jnp.bfloat16
    )
    width = projection.shape[0]
    replica = lax.axis_index("dp")
    partial_grad = lax.dot_general(
        lax.all_gather(projected, "tensor", axis=0, tiled=True),
        cotangent,
        (((0,), (0,)), ((), ())),
        preferred_element_type=jnp.float32,
    )
    grad = sum_at_owner(partial_grad, "dp", 0)
    t_value = step_count[0].astype(jnp.float32)
    new_first = 0.9 * first_moment + 0.1 * grad
    new_second = 0.999 * second_moment + 0.001 * grad * grad
    first_hat = new_first / (1.0 - jnp.power(jnp.float32(0.9), t_value))
    second_hat = new_second / (1.0 - jnp.power(jnp.float32(0.999), t_value))
    normalized = (first_hat / (jnp.sqrt(second_hat) + 1e-08)).astype(jnp.bfloat16)
    whole_steps = gather_directly(normalized, "dp", 0)
    out_rows = width // lax.axis_size("dp")
    local_projection = lax.dynamic_slice_in_dim(projection, replica * out_rows, out_rows, 0)
    update = jnp.dot(local_projection, whole_steps, preferred_element_type=jnp.float32).astype(
        jnp.bfloat16
    )
    return (update, new_first, new_second)


def solution(mesh):
    in_specs = (
        P(("dp", "tensor"), None),
        P("dp", "tensor"),
        P(),
        P("dp", "tensor"),
        P("dp", "tensor"),
        P(),
    )
    out_specs = (P("dp", "tensor"), P("dp", "tensor"), P("dp", "tensor"))
    return jax.shard_map(
        per_device, mesh=mesh, in_specs=in_specs, out_specs=out_specs, check_vma=False
    )
```

profile of v0, /device:TPU:1, one launch (start us, length us, event | category | flops | bytes accessed | tf_op | source)
XLA Modules:
  0.0 154.9 jit_solution(16666026992883483268)
XLA Ops:
  7.2 0.0 all-gather.2.cloned.1.call-start
  7.2 6.6 %convolution_convert_fusion.1 = bf16[512,512]{1,0:T(8,128)(2,1)} fusion(bf16[512,4096]{1,0:T(8,128)(2,1)} %param.6, bf16[4096,512]{1,0:T(8,128)(2,1)} %param.8), kind=kOutput, calls=%fused_computation.1 | convolution fusion | flops 2147745792 | bytes 8912896 | tf_op jit(solution)/shard_map/dot_general | solution.py:36
  13.8 0.0 all-gather.2.cloned.1.call-update
  13.8 74.0 %all-gather.2.cloned.1.call-done = bf16[8192,512]{1,0:T(8,128)(2,1)} async-done(((bf16[512,512]{1,0:T(8,128)(2,1)}), bf16[8192,512]{1,0:T(8,128)(2,1)}) %all-gather.2.cloned.1.call-update) | async-done | bytes 8388624 | tf_op jit(solution)/shard_map/all_gather | solution.py:42
  87.8 13.3 %fusion.4 = f32[512,688]{1,0:T(8,128)} fusion(bf16[8192,512]{1,0:T(8,128)(2,1)} %all-gather.2.cloned.1.call-done, bf16[8192,688]{0,1:T(8,128)(2,1)} %param.7), kind=kOutput, calls=%fused_computation.8 | convolution fusion | flops 5771362304 | bytes 21069824 | tf_op jit(solution)/shard_map/dot_general | solution.py:41
  101.1 0.0 copy-start
  101.1 0.0 copy-start.1
  101.1 5.2 %all-to-all-start = ((f32[8,64,688]{2,1,0:T(8,128)}), f32[8,64,688]{2,1,0:T(8,128)S(1)}, u32[]{:S(2)}, u32[]{:S(2)}) async-start(f32[8,64,688]{2,1,0:T(8,128)} %bitcast), calls=%async_computation | async-start | bytes 3145728 | tf_op jit(solution)/shard_map/all_to_all | solution.py:14
  107.1 20.0 %all-to-all-done = f32[8,64,688]{2,1,0:T(8,128)S(1)} async-done(((f32[8,64,688]{2,1,0:T(8,128)}), f32[8,64,688]{2,1,0:T(8,128)S(1)}, u32[]{:S(2)}, u32[]{:S(2)}) %all-to-all-start) | async-done | bytes 1409056 | tf_op jit(solution)/shard_map/all_to_all | solution.py:14
  127.1 0.1 reduce_sum.9
  127.2 0.0 copy-done
  127.2 0.0 copy-done.1
  127.2 0.9 divide_convert_fusion
  128.0 0.9 broadcast_in_dim.2
  129.0 4.3 %all-to-all-start.1 = ((bf16[8,64,688]{2,1,0:T(8,128)(2,1)}), bf16[8,64,688]{2,1,0:T(8,128)(2,1)S(1)}, u32[]{:S(2)}, u32[]{:S(2)}) async-start(bf16[8,64,688]{2,1,0:T(8,128)(2,1)} %broadcast_in_dim.2), calls=%async_computation.1 | async-start | bytes 1572864 | tf_op jit(solution)/shard_map/all_to_all | solution.py:26
  133.3 12.3 %all-to-all-done.1 = bf16[8,64,688]{2,1,0:T(8,128)(2,1)S(1)} async-done(((bf16[8,64,688]{2,1,0:T(8,128)(2,1)}), bf16[8,64,688]{2,1,0:T(8,128)(2,1)S(1)}, u32[]{:S(2)}, u32[]{:S(2)}) %all-to-all-start.1) | async-done | bytes 704544 | tf_op jit(solution)/shard_map/all_to_all | solution.py:26
  145.6 2.5 %convolution_convert_fusion = bf16[512,688]{0,1:T(8,128)(2,1)} fusion(bf16[512,688]{1,0:T(8,128)(2,1)S(1)} %bitcast.9, bf16[4096,512]{1,0:T(8,128)(2,1)} %param.8, s32[]{:T(128)S(6)} %select_n.3), kind=kOutput, calls=%fused_computation | convolution fusion | flops 361062400 | bytes 1933316 | tf_op jit(solution)/shard_map/dot_general | solution.py:57
Async XLA Ops:
  7.2 80.6 %all-gather.2.cloned.1.call-start = ((), (), s32[]{:S(2)}) async-start(), calls=%async_computation.2 | async-start | bytes 8912896 | tf_op jit(solution)/shard_map/all_gather | solution.py:42
  101.1 26.0 %copy-start = (f32[64,688]{1,0:T(8,128)S(1)}, f32[64,688]{1,0:T(8,128)}, u32[]{:S(2)}) copy-start(f32[64,688]{1,0:T(8,128)} %param.10) | copy-start | bytes 528388
  101.1 26.1 %copy-start.1 = (f32[64,688]{1,0:T(8,128)S(1)}, f32[64,688]{1,0:T(8,128)}, u32[]{:S(2)}) copy-start(f32[64,688]{1,0:T(8,128)} %param.9) | copy-start | bytes 528388
  101.1 25.9 %all-to-all-start = ((f32[8,64,688]{2,1,0:T(8,128)}), f32[8,64,688]{2,1,0:T(8,128)S(1)}, u32[]{:S(2)}, u32[]{:S(2)}) async-start(f32[8,64,688]{2,1,0:T(8,128)} %bitcast), calls=%async_computation | async-start | bytes 3145728 | tf_op jit(solution)/shard_map/all_to_all | solution.py:14
  129.0 16.6 %all-to-all-start.1 = ((bf16[8,64,688]{2,1,0:T(8,128)(2,1)}), bf16[8,64,688]{2,1,0:T(8,128)(2,1)S(1)}, u32[]{:S(2)}, u32[]{:S(2)}) async-start(bf16[8,64,688]{2,1,0:T(8,128)(2,1)} %broadcast_in_dim.2), calls=%async_computation.1 | async-start | bytes 1572864 | tf_op jit(solution)/shard_map/all_to_all | solution.py:26
Sparse Core Ops, SparseCore 0:
  13.9 73.8 all-gather.1
where the time goes:
time: 155 us
  waiting for transfers between devices  106 us (68%)
  matrix products  22.4 us (14%)
  between operations  14.8 us (10%)
  starting transfers between devices  9.59 us (6%)
    all_gather x1, waiting for transfers between devices, per_device(): lax.all_gather(projected, 'tensor', axis=0, tiled=True)  74 us
    all_to_all x1, waiting for transfers between devices, sum_at_owner(): parts = lax.all_to_all(in_blocks(shard, dim, count), axis, 0, 0, tiled=True)  20 us
    dot_general x1, matrix products, per_device(): lax.dot_general(lax.all_gather(projected, 'tensor', axis=0, tiled=True),...  13.3 us
    all_to_all x1, waiting for transfers between devices, sent_to_all(): lax.all_to_all(jnp.broadcast_to(shard[None], (count, *shard.shape)), axis...  12.3 us
    dot_general x1, matrix products, per_device(): jnp.dot(activations, projection, preferred_element_type=jnp.float32)  6.59 us
    all_to_all x1, starting transfers between devices, sum_at_owner(): parts = lax.all_to_all(in_blocks(shard, dim, count), axis, 0, 0, tiled=True)  5.23 us
    all_to_all x1, starting transfers between devices, sent_to_all(): lax.all_to_all(jnp.broadcast_to(shard[None], (count, *shard.shape)), axis...  4.32 us
  transfers between devices with their start and end apart: 3, of which 3 were waited for; matrix products, arithmetic and copies ran while one was open for 0% of the time, Pallas kernels for 0%

commit v1 on v0

v1 whole, which is shorter than its diff:
```python
import functools

import jax
import jax.numpy as jnp
from jax import lax
from jax.experimental import pallas as pl
from jax.experimental.pallas import tpu as pltpu
from jax.sharding import PartitionSpec as P

MESH = pl.DeviceIdType.MESH
BF, F32 = jnp.bfloat16, jnp.float32
D, F, R = 4096, 11008, 512
TOK = 512
HALF = TOK // 2
NX, NY, NDP = 4, 4, 8
NT = NX * NY
FC = F // NT
DR = D // NDP
PER = R // NDP
CHUNKS = (128, 128, 128, 128)
SHARES = tuple(c // NDP for c in CHUNKS)
STARTS = tuple(sum(SHARES[:i]) for i in range(len(CHUNKS)))
NC = len(CHUNKS)
KSTEPS = 4
KW = D // KSTEPS
GROUP = 4 * HALF
OFFSETS = (0, -1, 1, 2)


def dot(a, b, ca, cb):
    return lax.dot_general(a, b, (((ca,), (cb,)), ((), ())), preferred_element_type=F32)


def identity():
    rows = lax.broadcasted_iota(jnp.int32, (R, R), 0)
    cols = lax.broadcasted_iota(jnp.int32, (R, R), 1)
    return jnp.where(rows == cols, 1.0, 0.0).astype(BF)


def kernel(
    act_hbm, cot_hbm, proj_hbm, first_hbm, second_hbm, step_ref,
    upd_hbm, nfirst_hbm, nsecond_hbm,
    act, proj, cot, first, second, nfirst, nsecond, eye, projt, upd_acc, upd_out,
    *rest,
):
    gath, acc = rest[:NC], rest[NC : 2 * NC]
    part, parts_in = rest[2 * NC : 3 * NC], rest[3 * NC : 4 * NC]
    steps = rest[4 * NC : 5 * NC]
    load_sem, cot_sem, store_sem, ssem, rsem, part_ssem, part_rsem, step_ssem, step_rsem = rest[5 * NC :]

    d = lax.axis_index("dp")
    t = lax.axis_index("tensor")
    y, x = t // NX, t % NX
    pos = ((x, y), (y, x))

    def dev(axis, off):
        if axis == 0:
            return {"dp": d, "tensor": y * NX + (x + off + NX) % NX}
        return {"dp": d, "tensor": ((y + off + NY) % NY) * NX + x}

    def peer(j):
        return {"dp": (d + j) % NDP, "tensor": t}

    loads = []
    for k in range(KSTEPS):
        loads.append(pltpu.make_async_copy(act_hbm.at[:, pl.ds(k * KW, KW)], act.at[:, pl.ds(k * KW, KW)], load_sem.at[2 * k]))
        loads.append(pltpu.make_async_copy(proj_hbm.at[pl.ds(k * KW, KW)], proj.at[pl.ds(k * KW, KW)], load_sem.at[2 * k + 1]))
    loads.append(pltpu.make_async_copy(first_hbm, first, load_sem.at[2 * KSTEPS]))
    loads.append(pltpu.make_async_copy(second_hbm, second, load_sem.at[2 * KSTEPS + 1]))
    for c in loads[: 2 * KSTEPS]:
        c.start()

    barrier = pltpu.get_barrier_semaphore()
    for axis in (0, 1):
        for off in (1, -1):
            pl.semaphore_signal(barrier, inc=1, device_id=dev(axis, off), device_id_type=MESH)
    for j in range(1, NDP):
        pl.semaphore_signal(barrier, inc=1, device_id=peer(j), device_id_type=MESH)

    cot_loads = {}
    for h in (0, 1):
        for v in range(4):
            for u in range(4):
                tt = v * NX + u if h == 0 else u * NX + v
                cot_loads[h, v, u] = pltpu.make_async_copy(
                    cot_hbm.at[:, pl.ds(tt * TOK + h * HALF, HALF)],
                    cot.at[h, v, u],
                    cot_sem.at[h, v, u],
                )
    eye[...] = identity()

    def block(c, h, u, v, q):
        first_pos, second_pos = pos[h]
        ref = gath[c].at[h, (second_pos + v + 4) % 4, (first_pos + u + 4) % 4]
        if q is not None:
            ref = ref.at[pl.ds(q * (CHUNKS[c] // 2), CHUNKS[c] // 2)]
        return ref

    def send(c, h, i, order, off, u, v, q):
        ref = block(c, h, u, v, q)
        pltpu.make_async_remote_copy(
            ref, ref, ssem.at[c, h, i], rsem.at[c, h, i],
            device_id=dev(order ^ h, off), device_id_type=MESH,
        ).start()

    def arrived(c, h, i, u, v, q):
        ref = block(c, h, u, v, q)
        pltpu.make_async_copy(ref, ref, rsem.at[c, h, i]).wait()

    def own_first(c, h):
        send(c, h, 0, 0, 1, 0, 0, None)
        send(c, h, 1, 0, -1, 0, 0, None)

    def to_second(c, h, k):
        send(c, h, 4 + 4 * k, 1, 1, OFFSETS[k], 0, None)
        send(c, h, 5 + 4 * k, 1, -1, OFFSETS[k], 0, None)

    def pass_first(c):
        for h in (0, 1):
            arrived(c, h, 0, -1, 0, None)
            send(c, h, 2, 0, 1, -1, 0, 0)
            arrived(c, h, 1, 1, 0, None)
            send(c, h, 3, 0, -1, 1, 0, 1)
        for h in (0, 1):
            to_second(c, h, 1)
            to_second(c, h, 2)

    def far_first(c):
        for h in (0, 1):
            arrived(c, h, 2, 2, 0, 0)
            arrived(c, h, 3, 2, 0, 1)
            to_second(c, h, 3)

    def pass_second(c, h, k):
        arrived(c, h, 4 + 4 * k, OFFSETS[k], -1, None)
        send(c, h, 6 + 4 * k, 1, 1, OFFSETS[k], -1, 0)
        arrived(c, h, 5 + 4 * k, OFFSETS[k], 1, None)
        send(c, h, 7 + 4 * k, 1, -1, OFFSETS[k], 1, 1)

    def far_second(c, h):
        for k in range(4):
            arrived(c, h, 6 + 4 * k, OFFSETS[k], 2, 0)
            arrived(c, h, 7 + 4 * k, OFFSETS[k], 2, 1)

    def sent(c):
        for h in (0, 1):
            for i in range(20):
                whole = i in (0, 1) or (i >= 4 and i % 4 in (0, 1))
                ref = block(c, h, 0, 0, None if whole else 0)
                pltpu.make_async_copy(ref, ref, ssem.at[c, h, i]).wait()

    def add_group(c, h, v, fresh=False):
        place = (pos[h][1] + v + 4) % 4
        p = jnp.concatenate([gath[c][h, place, u] for u in range(4)], axis=1)
        g = jnp.concatenate([cot[h, place, u] for u in range(4)], axis=1)
        value = dot(p, g, 1, 1)
        if fresh:
            acc[c][...] = value
        else:
            acc[c][...] += value

    def part_copy(c, j):
        return pltpu.make_async_remote_copy(
            part[c].at[(d + j) % NDP], parts_in[c].at[j - 1], part_ssem.at[c, j - 1], part_rsem.at[c, j - 1],
            device_id=peer(j), device_id_type=MESH,
        )

    def step_copy(c, j):
        return pltpu.make_async_remote_copy(
            steps[c].at[d], steps[c].at[d], step_ssem.at[c, j - 1], step_rsem.at[c, j - 1],
            device_id=peer(j), device_id_type=MESH,
        )

    def share_parts(c):
        share = SHARES[c]
        part[c][...] = acc[c][...].reshape(NDP, share, FC).astype(BF)
        for j in range(1, NDP):
            part_copy(c, j).start()

    def adam(c):
        share, start = SHARES[c], STARTS[c]
        t_value = jnp.full((8, 128), step_ref[0].astype(F32), F32)
        fix_first = (1.0 / (1.0 - jnp.power(jnp.full((8, 128), 0.9, F32), t_value)))[0:1, 0:1]
        fix_second = (1.0 / (1.0 - jnp.power(jnp.full((8, 128), 0.999, F32), t_value)))[0:1, 0:1]
        grad = acc[c][pl.ds(pl.multiple_of(d * share, share), share), :]
        for j in range(1, NDP):
            part_copy(c, j).wait_recv()
            grad = grad + parts_in[c][j - 1].astype(F32)
        rows = pl.ds(start, share)
        new_first = 0.9 * first[rows, :] + 0.1 * grad
        new_second = 0.999 * second[rows, :] + 0.001 * grad * grad
        nfirst[rows, :] = new_first
        nsecond[rows, :] = new_second
        normalized = (new_first * fix_first) / (jnp.sqrt(new_second * fix_second) + 1e-08)
        steps[c][d] = normalized.astype(BF)
        for j in range(1, NDP):
            step_copy(c, j).start()

    def update(c):
        for j in range(1, NDP):
            step_copy(c, j).wait_recv()
        chunk = steps[c][...].astype(F32).reshape(CHUNKS[c], FC)
        value = dot(chunk.T.astype(BF), projt[pl.ds(sum(CHUNKS[:c]), CHUNKS[c]), :], 1, 0)
        if c == 0:
            upd_acc[...] = value
        elif c < NC - 1:
            upd_acc[...] += value
        else:
            upd_out[...] = (upd_acc[...] + value).astype(BF)

    for h in (0, 1):
        total = None
        for k in range(KSTEPS):
            if h == 0:
                loads[2 * k].wait()
                loads[2 * k + 1].wait()
            value = dot(act[pl.ds(h * HALF, HALF), pl.ds(k * KW, KW)], proj[pl.ds(k * KW, KW), :], 1, 0)
            total = value if total is None else total + value
        turned = dot(eye[...], total.astype(BF), 1, 1)
        for c in range(NC):
            rows = [turned[PER * e + STARTS[c] : PER * e + STARTS[c] + SHARES[c]] for e in range(NDP)]
            gath[c][h, pos[h][1], pos[h][0]] = jnp.concatenate(rows, axis=0).astype(BF)
        if h == 0:
            pl.semaphore_wait(barrier, 4 + NDP - 1)
            for c in loads[2 * KSTEPS :]:
                c.start()
            for c in cot_loads.values():
                c.start()
        for c in range(NC):
            own_first(c, h)
            if c < 2:
                to_second(c, h, 0)
    turned = dot(eye[...], proj[pl.ds(pl.multiple_of(d * DR, DR), DR), :], 1, 1)
    for c in range(NC):
        rows = [turned[PER * e + STARTS[c] : PER * e + STARTS[c] + SHARES[c]] for e in range(NDP)]
        projt[pl.ds(sum(CHUNKS[:c]), CHUNKS[c]), :] = jnp.concatenate(rows, axis=0).astype(BF)

    for i in range(NC + 2):
        if i < NC:
            pass_first(i)
            far_first(i)
            if 2 <= i + 1 < NC:
                for h in (0, 1):
                    to_second(i + 1, h, 0)
            if i == 0:
                for c in loads[2 * KSTEPS :]:
                    c.wait()
                for c in cot_loads.values():
                    c.wait()
        c = i - 1
        if 0 <= c < NC:
            for h in (0, 1):
                for k in range(4):
                    pass_second(c, h, k)
        if i < NC:
            add_group(i, 0, 0, fresh=True)
            add_group(i, 1, 0)
        if 0 <= c < NC:
            for h in (0, 1):
                add_group(c, h, -1)
                add_group(c, h, 1)
        c = i - 2
        if 0 <= c < NC:
            for h in (0, 1):
                far_second(c, h)
                add_group(c, h, 2)
            share_parts(c)
        if 0 <= c - 1:
            adam(c - 1)
        if 0 <= c - 2:
            update(c - 2)
    for c in range(NC):
        sent(c)
    update(NC - 2)
    for c in range(NC - 1):
        for j in range(1, NDP):
            part_copy(c, j).wait_send()
            step_copy(c, j).wait_send()
    adam(NC - 1)
    stores = [
        pltpu.make_async_copy(nfirst, nfirst_hbm, store_sem.at[0]),
        pltpu.make_async_copy(nsecond, nsecond_hbm, store_sem.at[1]),
        pltpu.make_async_copy(upd_out, upd_hbm, store_sem.at[2]),
    ]
    stores[0].start()
    stores[1].start()
    update(NC - 1)
    stores[2].start()
    for j in range(1, NDP):
        part_copy(NC - 1, j).wait_send()
        step_copy(NC - 1, j).wait_send()
    for c in stores:
        c.wait()


def per_device(activations, cotangent, projection, first_moment, second_moment, step_count):
    anywhere = pl.BlockSpec(memory_space=pl.ANY)
    scratch = [
        pltpu.VMEM((TOK, D), BF),
        pltpu.VMEM((D, R), BF),
        pltpu.VMEM((2, 4, 4, FC, HALF), BF),
        pltpu.VMEM((PER, FC), F32),
        pltpu.VMEM((PER, FC), F32),
        pltpu.VMEM((PER, FC), F32),
        pltpu.VMEM((PER, FC), F32),
        pltpu.VMEM((R, R), BF),
        pltpu.VMEM((R, DR), BF),
        pltpu.VMEM((FC, DR), F32),
        pltpu.VMEM((FC, DR), BF),
    ]
    scratch += [pltpu.VMEM((2, 4, 4, c, HALF), BF) for c in CHUNKS]
    scratch += [pltpu.VMEM((c, FC), F32) for c in CHUNKS]
    scratch += [pltpu.VMEM((NDP, s, FC), BF) for s in SHARES]
    scratch += [pltpu.VMEM((NDP - 1, s, FC), BF) for s in SHARES]
    scratch += [pltpu.VMEM((NDP, s, FC), BF) for s in SHARES]
    dma = pltpu.SemaphoreType.DMA
    scratch += [
        dma((2 * KSTEPS + 2,)), dma((2, 4, 4)), dma((3,)), dma((NC, 2, 20)), dma((NC, 2, 20)),
        dma((NC, NDP - 1)), dma((NC, NDP - 1)), dma((NC, NDP - 1)), dma((NC, NDP - 1)),
    ]
    update_t, new_first, new_second = pl.pallas_call(
        kernel,
        out_shape=(
            jax.ShapeDtypeStruct((FC, DR), BF),
            jax.ShapeDtypeStruct((PER, FC), F32),
            jax.ShapeDtypeStruct((PER, FC), F32),
        ),
        in_specs=[anywhere] * 5 + [pl.BlockSpec(memory_space=pltpu.SMEM)],
        out_specs=[anywhere] * 3,
        scratch_shapes=scratch,
        compiler_params=pltpu.CompilerParams(
            collective_id=0, has_side_effects=True, vmem_limit_bytes=56 * 2**20
        ),
        cost_estimate=pl.CostEstimate(flops=9 * 10**9, bytes_accessed=25 * 10**6, transcendentals=0),
    )(activations, cotangent.T, projection, first_moment, second_moment, step_count)
    return update_t.T, new_first, new_second


def solution(mesh):
    in_specs = (
        P(("dp", "tensor"), None),
        P("dp", "tensor"),
        P(),
        P("dp", "tensor"),
        P("dp", "tensor"),
        P(),
    )
    out_specs = (P("dp", "tensor"), P("dp", "tensor"), P("dp", "tensor"))
    return jax.shard_map(
        per_device, mesh=mesh, in_specs=in_specs, out_specs=out_specs, check_vma=False
    )
```

time: 155 us -> 81.8 us (0.53)
  waiting for transfers between devices: 106 us -> 0 us
  Pallas kernels: 0 us -> 75.1 us
  matrix products: 22.4 us -> 0 us
  between operations: 14.8 us -> 1.29 us
  starting transfers between devices: 9.59 us -> 0 us
  local copies, waits for them, and re-layouts: 0.94 us -> 5.23 us
    pallas_call x0 -> x1, Pallas kernels: none -> 75.1 us  [per_device(): pl.pallas_call(kernel, out_shape=(jax.ShapeDtypeStruct((FC, DR), BF), jax...]
    all_gather x1 -> x0, waiting for transfers between devices: 74 us -> none  [per_device(): lax.all_gather(projected, 'tensor', axis=0, tiled=True)]
    all_to_all x2 -> x0, waiting for transfers between devices: 32.3 us -> none  [the longest x1 20 us: sum_at_owner(): parts = lax.all_to_all(in_blocks(shard, dim, count), axis, 0, 0, tiled=True)]
    dot_general x3 -> x0, matrix products: 22.4 us -> none  [the longest x1 13.3 us: per_device(): lax.dot_general(lax.all_gather(projected, 'tensor', axis=0, tiled=True),...]
    all_to_all x2 -> x0, starting transfers between devices: 9.55 us -> none  [the longest x1 5.23 us: sum_at_owner(): parts = lax.all_to_all(in_blocks(shard, dim, count), axis, 0, 0, tiled=True)]
    unnamed x4 -> x3, local copies, waits for them, and re-layouts: 0.01 us -> 5.23 us
  transfers between devices with their start and end apart: 3 -> 0, of which waited for: 3 -> 0; matrix products, arithmetic and copies ran while one was open for 0% -> 0% of each run, Pallas kernels for 0% -> 0%
where the time goes in v1:
time: 81.8 us; the launch traced here: 81.6 us
  Pallas kernels  75.1 us (92%)
  local copies, waits for them, and re-layouts  5.23 us (6%)
  between operations  1.29 us (2%)
    pallas_call x1, Pallas kernels, per_device(): pl.pallas_call(kernel, out_shape=(jax.ShapeDtypeStruct((FC, DR), BF), jax...  75.1 us
    unnamed x3, local copies, waits for them, and re-layouts  5.23 us

profile of v1, /device:TPU:1, one launch (start us, length us, event | category | flops | bytes accessed | tf_op | source)
XLA Modules:
  0.0 81.6 jit_solution(4515893779960941076)
XLA Ops:
  1.3 75.1 %shard_map.85 = (bf16[688,512]{1,0:T(8,128)(2,1)}, f32[64,688]{1,0:T(8,128)}, f32[64,688]{1,0:T(8,128)}) custom-call(bf16[512,4096]{1,0:T(8,128)(2,1)} %act_hbm.1, bf16[688,8192]{1,0:T(8,128)(2,1)} %bitcast.3, bf16[4096,512]{1,0:T(8,128)(2,1)} %proj_hbm.1, f32[64,688]{1,0:T(8,128)} %first_hbm.1, f32[64,688]{1,0:T(8,128)} %second_hbm.1, s32[1]{0:T(128)S(6)} %copy.12.step_ref), custom_call_target="tpu_custom_call" | custom-call | flops 8999999488 | bytes 25000000 | tf_op jit(solution)/shard_map/pallas_call | solution.py:321
  76.4 2.0 %copy.13 = bf16[512,688]{0,1:T(8,128)(2,1)} copy(bf16[512,688]{0,1:T(8,128)(2,1)} %bitcast.2) | data formatting | bytes 1409024
  78.4 1.6 %copy.14 = f32[64,688]{1,0:T(8,128)} copy(f32[64,688]{1,0:T(8,128)} %get-tuple-element.13) | data formatting | bytes 352256
  80.0 1.6 %copy.15 = f32[64,688]{1,0:T(8,128)} copy(f32[64,688]{1,0:T(8,128)} %get-tuple-element.14) | data formatting | bytes 352256

commit v2 on v1

v2 whole, which is shorter than its diff:
```python
import functools

import jax
import jax.numpy as jnp
from jax import lax
from jax.experimental import pallas as pl
from jax.experimental.pallas import tpu as pltpu
from jax.sharding import PartitionSpec as P

MESH = pl.DeviceIdType.MESH
BF, F32 = jnp.bfloat16, jnp.float32
D, F, R = 4096, 11008, 512
TOK = 512
HALF = TOK // 2
NX, NY, NDP = 4, 4, 8
NT = NX * NY
FC = F // NT
DR = D // NDP
PER = R // NDP
CHUNKS = (128, 128, 128, 128)
SHARES = tuple(c // NDP for c in CHUNKS)
STARTS = tuple(sum(SHARES[:i]) for i in range(len(CHUNKS)))
NC = len(CHUNKS)
KSTEPS = 4
KW = D // KSTEPS
GROUP = 4 * HALF
VMEM_MIB = 52
OFFSETS = (0, -1, 1, 2)


def dot(a, b, ca, cb):
    return lax.dot_general(a, b, (((ca,), (cb,)), ((), ())), preferred_element_type=F32)


def identity():
    rows = lax.broadcasted_iota(jnp.int32, (R, R), 0)
    cols = lax.broadcasted_iota(jnp.int32, (R, R), 1)
    return jnp.where(rows == cols, 1.0, 0.0).astype(BF)


def kernel(
    act_hbm, cot_hbm, proj_hbm, first_hbm, second_hbm, step_hbm,
    upd_out, nfirst, nsecond,
    step_now, act, proj, cot, first, second, eye, projt, upd_acc,
    *rest,
):
    gath, acc = rest[:NC], rest[NC : 2 * NC]
    part, parts_in = rest[2 * NC : 3 * NC], rest[3 * NC : 4 * NC]
    steps = rest[4 * NC : 5 * NC]
    load_sem, cot_sem, ssem, rsem, part_ssem, part_rsem, step_ssem, step_rsem = rest[5 * NC :]

    d = lax.axis_index("dp")
    t = lax.axis_index("tensor")
    y, x = t // NX, t % NX
    pos = ((x, y), (y, x))

    def dev(axis, off):
        if axis == 0:
            return {"dp": d, "tensor": y * NX + (x + off + NX) % NX}
        return {"dp": d, "tensor": ((y + off + NY) % NY) * NX + x}

    def peer(j):
        return {"dp": (d + j) % NDP, "tensor": t}

    loads = []
    for k in range(KSTEPS):
        loads.append(pltpu.make_async_copy(act_hbm.at[:, pl.ds(k * KW, KW)], act.at[:, pl.ds(k * KW, KW)], load_sem.at[2 * k]))
        loads.append(pltpu.make_async_copy(proj_hbm.at[pl.ds(k * KW, KW)], proj.at[pl.ds(k * KW, KW)], load_sem.at[2 * k + 1]))
    loads.append(pltpu.make_async_copy(first_hbm, first, load_sem.at[2 * KSTEPS]))
    loads.append(pltpu.make_async_copy(second_hbm, second, load_sem.at[2 * KSTEPS + 1]))
    loads.append(pltpu.make_async_copy(step_hbm, step_now, load_sem.at[2 * KSTEPS + 2]))
    for c in loads[: 2 * KSTEPS]:
        c.start()

    barrier = pltpu.get_barrier_semaphore()
    for axis in (0, 1):
        for off in (1, -1):
            pl.semaphore_signal(barrier, inc=1, device_id=dev(axis, off), device_id_type=MESH)
    for j in range(1, NDP):
        pl.semaphore_signal(barrier, inc=1, device_id=peer(j), device_id_type=MESH)

    cot_loads = {}
    for h in (0, 1):
        for v in range(4):
            for u in range(4):
                tt = v * NX + u if h == 0 else u * NX + v
                cot_loads[h, v, u] = pltpu.make_async_copy(
                    cot_hbm.at[:, pl.ds(tt * TOK + h * HALF, HALF)],
                    cot.at[h, v * 4 + u],
                    cot_sem.at[0],
                )
    eye[...] = identity()

    def place(h, u, v):
        first_pos, second_pos = pos[h]
        return ((second_pos + v + 4) % 4) * 4 + (first_pos + u + 4) % 4

    def send(c, h, i, order, off, u, v, q):
        ref = gath[c].at[h, place(h, u, v)]
        if q is not None:
            ref = ref.at[pl.ds(q * (CHUNKS[c] // 2), CHUNKS[c] // 2)]
        pltpu.make_async_remote_copy(
            ref, ref, ssem.at[c, h], rsem.at[c, h, i],
            device_id=dev(order ^ h, off), device_id_type=MESH,
        ).start()

    def arrived(c, h, i, blocks):
        ref = gath[c].at[h, pl.ds(0, blocks)]
        pltpu.make_async_copy(ref, ref, rsem.at[c, h, i]).wait()

    def own_first(c, h):
        send(c, h, 0, 0, 1, 0, 0, None)
        send(c, h, 0, 0, -1, 0, 0, None)

    def to_second(c, h, k):
        send(c, h, 2 + k, 1, 1, OFFSETS[k], 0, None)
        send(c, h, 2 + k, 1, -1, OFFSETS[k], 0, None)

    def pass_first(c):
        for h in (0, 1):
            arrived(c, h, 0, 2)
            send(c, h, 1, 0, 1, -1, 0, 0)
            send(c, h, 1, 0, -1, 1, 0, 1)

    def far_first(c):
        for h in (0, 1):
            arrived(c, h, 1, 1)

    def pass_second(c, h, k):
        arrived(c, h, 2 + k, 2)
        send(c, h, 6, 1, 1, OFFSETS[k], -1, 0)
        send(c, h, 6, 1, -1, OFFSETS[k], 1, 1)

    def far_second(c, h):
        arrived(c, h, 6, 4)

    def sent(c):
        for h in (0, 1):
            ref = gath[c].at[h, pl.ds(0, 15)]
            pltpu.make_async_copy(ref, ref, ssem.at[c, h]).wait()

    def add_group(c, h, v, fresh=False):
        at = ((pos[h][1] + v + 4) % 4) * 4
        p = jnp.concatenate([gath[c][h, at + u] for u in range(4)], axis=1)
        g = jnp.concatenate([cot[h, at + u] for u in range(4)], axis=1)
        value = dot(p, g, 1, 1)
        if fresh:
            acc[c][...] = value
        else:
            acc[c][...] += value

    def part_copy(c, j):
        return pltpu.make_async_remote_copy(
            part[c].at[(d + j) % NDP], parts_in[c].at[j - 1], part_ssem.at[c], part_rsem.at[c],
            device_id=peer(j), device_id_type=MESH,
        )

    def step_copy(c, j):
        return pltpu.make_async_remote_copy(
            steps[c].at[d], steps[c].at[d], step_ssem.at[c], step_rsem.at[c],
            device_id=peer(j), device_id_type=MESH,
        )

    def share_parts(c):
        share = SHARES[c]
        part[c][...] = acc[c][...].reshape(NDP, share, FC).astype(BF)
        for j in range(1, NDP):
            part_copy(c, j).start()

    def adam(c):
        share, start = SHARES[c], STARTS[c]
        t_value = jnp.full((8, 128), step_now[0].astype(F32), F32)
        fix_first = (1.0 / (1.0 - jnp.power(jnp.full((8, 128), 0.9, F32), t_value)))[0:1, 0:1]
        fix_second = (1.0 / (1.0 - jnp.power(jnp.full((8, 128), 0.999, F32), t_value)))[0:1, 0:1]
        grad = acc[c][pl.ds(pl.multiple_of(d * share, share), share), :]
        pltpu.make_async_copy(parts_in[c], parts_in[c], part_rsem.at[c]).wait()
        for j in range(1, NDP):
            grad = grad + parts_in[c][j - 1].astype(F32)
        rows = pl.ds(start, share)
        new_first = 0.9 * first[rows, :] + 0.1 * grad
        new_second = 0.999 * second[rows, :] + 0.001 * grad * grad
        nfirst[rows, :] = new_first
        nsecond[rows, :] = new_second
        normalized = (new_first * fix_first) / (jnp.sqrt(new_second * fix_second) + 1e-08)
        steps[c][d] = normalized.astype(BF)
        for j in range(1, NDP):
            step_copy(c, j).start()

    def update(c):
        seven = steps[c].at[pl.ds(0, NDP - 1)]
        pltpu.make_async_copy(seven, seven, step_rsem.at[c]).wait()
        chunk = steps[c][...].astype(F32).reshape(CHUNKS[c], FC)
        value = dot(chunk.T.astype(BF), projt[pl.ds(sum(CHUNKS[:c]), CHUNKS[c]), :], 1, 0)
        if c == 0:
            upd_acc[...] = value
        elif c < NC - 1:
            upd_acc[...] += value
        else:
            upd_out[...] = (upd_acc[...] + value).astype(BF)

    for h in (0, 1):
        total = None
        for k in range(KSTEPS):
            if h == 0:
                loads[2 * k].wait()
                loads[2 * k + 1].wait()
            value = dot(act[pl.ds(h * HALF, HALF), pl.ds(k * KW, KW)], proj[pl.ds(k * KW, KW), :], 1, 0)
            total = value if total is None else total + value
        turned = dot(eye[...], total.astype(BF), 1, 1)
        for c in range(NC):
            rows = [turned[PER * e + STARTS[c] : PER * e + STARTS[c] + SHARES[c]] for e in range(NDP)]
            gath[c][h, place(h, 0, 0)] = jnp.concatenate(rows, axis=0).astype(BF)
        if h == 0:
            pl.semaphore_wait(barrier, 4 + NDP - 1)
            for c in loads[2 * KSTEPS :]:
                c.start()
            for c in cot_loads.values():
                c.start()
        own_first(0, h)
        to_second(0, h, 0)
    for c in range(1, NC):
        for h in (0, 1):
            own_first(c, h)
    turned = dot(eye[...], proj[pl.ds(pl.multiple_of(d * DR, DR), DR), :], 1, 1)
    for c in range(NC):
        rows = [turned[PER * e + STARTS[c] : PER * e + STARTS[c] + SHARES[c]] for e in range(NDP)]
        projt[pl.ds(sum(CHUNKS[:c]), CHUNKS[c]), :] = jnp.concatenate(rows, axis=0).astype(BF)

    pass_first(0)
    for k in (1, 2):
        for h in (0, 1):
            to_second(0, h, k)
    for c in range(1, NC):
        pass_first(c)
    far_first(0)
    for h in (0, 1):
        to_second(0, h, 3)
    for c in range(1, NC):
        far_first(c)
    for c in loads[2 * KSTEPS :]:
        c.wait()
    pltpu.make_async_copy(cot, cot, cot_sem.at[0]).wait()

    for i in range(NC):
        if i + 1 < NC:
            for k in range(4):
                for h in (0, 1):
                    to_second(i + 1, h, k)
        for k in range(4):
            for h in (0, 1):
                pass_second(i, h, k)
            if k == 0:
                add_group(i, 0, 0, fresh=True)
            if k == 1:
                add_group(i, 1, 0)
                if i >= 2:
                    adam(i - 2)
            if k == 2 and i >= 3:
                update(i - 3)
        add_group(i, 0, -1)
        add_group(i, 0, 1)
        if i >= 1:
            for h in (0, 1):
                far_second(i - 1, h)
                add_group(i - 1, h, 2)
            share_parts(i - 1)
        add_group(i, 1, -1)
        add_group(i, 1, 1)
    for h in (0, 1):
        far_second(NC - 1, h)
        add_group(NC - 1, h, 2)
    share_parts(NC - 1)
    adam(NC - 2)
    update(NC - 3)
    for c in range(NC):
        sent(c)
    for c in range(NC - 1):
        pltpu.make_async_copy(parts_in[c], parts_in[c], part_ssem.at[c]).wait()
    adam(NC - 1)
    for c in range(NC - 1):
        seven = steps[c].at[pl.ds(0, NDP - 1)]
        pltpu.make_async_copy(seven, seven, step_ssem.at[c]).wait()
    update(NC - 2)
    update(NC - 1)
    pltpu.make_async_copy(parts_in[NC - 1], parts_in[NC - 1], part_ssem.at[NC - 1]).wait()
    seven = steps[NC - 1].at[pl.ds(0, NDP - 1)]
    pltpu.make_async_copy(seven, seven, step_ssem.at[NC - 1]).wait()


def write_out(*arrays):
    def body(*refs):
        n = len(arrays)
        copies = [
            pltpu.make_async_copy(refs[i], refs[n + i], refs[2 * n].at[i]) for i in range(n)
        ]
        for c in copies:
            c.start()
        for c in copies:
            c.wait()

    return pl.pallas_call(
        body,
        out_shape=tuple(jax.ShapeDtypeStruct(a.shape, a.dtype) for a in arrays),
        in_specs=[pl.BlockSpec(memory_space=pltpu.VMEM)] * len(arrays),
        out_specs=[pl.BlockSpec(memory_space=pltpu.HBM)] * len(arrays),
        scratch_shapes=[pltpu.SemaphoreType.DMA((len(arrays),))],
        compiler_params=pltpu.CompilerParams(vmem_limit_bytes=2 * 2**20),
    )(*arrays)


def per_device(activations, cotangent, projection, first_moment, second_moment, step_count):
    scratch = [
        pltpu.SMEM((1,), jnp.int32),
        pltpu.VMEM((TOK, D), BF),
        pltpu.VMEM((D, R), BF),
        pltpu.VMEM((2, NT, FC, HALF), BF),
        pltpu.VMEM((PER, FC), F32),
        pltpu.VMEM((PER, FC), F32),
        pltpu.VMEM((R, R), BF),
        pltpu.VMEM((R, DR), BF),
        pltpu.VMEM((FC, DR), F32),
    ]
    scratch += [pltpu.VMEM((2, NT, c, HALF), BF) for c in CHUNKS]
    scratch += [pltpu.VMEM((c, FC), F32) for c in CHUNKS]
    scratch += [pltpu.VMEM((NDP, s, FC), BF) for s in SHARES]
    scratch += [pltpu.VMEM((NDP - 1, s, FC), BF) for s in SHARES]
    scratch += [pltpu.VMEM((NDP, s, FC), BF) for s in SHARES]
    dma = pltpu.SemaphoreType.DMA
    scratch += [
        dma((2 * KSTEPS + 3,)), dma((1,)), dma((NC, 2)), dma((NC, 2, 7)),
        dma((NC,)), dma((NC,)), dma((NC,)), dma((NC,)),
    ]
    update_t, new_first, new_second = pl.pallas_call(
        kernel,
        out_shape=(
            jax.ShapeDtypeStruct((FC, DR), BF),
            jax.ShapeDtypeStruct((PER, FC), F32),
            jax.ShapeDtypeStruct((PER, FC), F32),
        ),
        in_specs=[pl.BlockSpec(memory_space=pltpu.HBM)] * 6,
        out_specs=[pl.BlockSpec(memory_space=pltpu.VMEM)] * 3,
        scratch_shapes=scratch,
        compiler_params=pltpu.CompilerParams(
            collective_id=0, has_side_effects=True, vmem_limit_bytes=int(VMEM_MIB * 2**20)
        ),
        cost_estimate=pl.CostEstimate(flops=9 * 10**9, bytes_accessed=25 * 10**6, transcendentals=0),
    )(activations, cotangent.T, projection, first_moment, second_moment, step_count)
    update_t, new_first, new_second = write_out(update_t, new_first, new_second)
    return update_t.T, new_first, new_second


def solution(mesh):
    in_specs = (
        P(("dp", "tensor"), None),
        P("dp", "tensor"),
        P(),
        P("dp", "tensor"),
        P("dp", "tensor"),
        P(),
    )
    out_specs = (P("dp", "tensor"), P("dp", "tensor"), P("dp", "tensor"))
    return jax.shard_map(
        per_device, mesh=mesh, in_specs=in_specs, out_specs=out_specs, check_vma=False
    )
```

time: 81.8 us -> 72.8 us (0.89)
  Pallas kernels: 75.1 us -> 69.5 us
  local copies, waits for them, and re-layouts: 5.23 us -> 1.85 us
    pallas_call x1, Pallas kernels: 75.1 us -> 68.5 us  [per_device(): pl.pallas_call(kernel, out_shape=(jax.ShapeDtypeStruct((FC, DR), BF), jax...]
    unnamed x3 -> x4, local copies, waits for them, and re-layouts: 5.23 us -> 1.85 us
    pallas_call x0 -> x1, Pallas kernels: none -> 1 us  [write_out(): pl.pallas_call(body, out_shape=tuple((jax.ShapeDtypeStruct(a.shape, a.dty...]
where the time goes in v2:
time: 72.8 us; the launch traced here: 72.6 us
  Pallas kernels  69.5 us (95%)
  local copies, waits for them, and re-layouts  1.85 us (3%)
  between operations  1.3 us (2%)
    pallas_call x1, Pallas kernels, per_device(): pl.pallas_call(kernel, out_shape=(jax.ShapeDtypeStruct((FC, DR), BF), jax...  68.5 us
    unnamed x4, local copies, waits for them, and re-layouts  1.85 us

profile of v2, /device:TPU:1, one launch (start us, length us, event | category | flops | bytes accessed | tf_op | source)
XLA Modules:
  0.0 72.6 jit_solution(7223559918416825710)
XLA Ops:
  1.3 0.0 copy-start
  1.3 0.9 %copy-done = f32[64,688]{1,0:T(8,128)S(1)} copy-done((f32[64,688]{1,0:T(8,128)S(1)}, f32[64,688]{1,0:T(8,128)}, u32[]{:S(2)}) %copy-start) | copy-done | bytes 176152
  2.2 0.0 copy-start.1
  2.2 0.9 %copy-done.1 = f32[64,688]{1,0:T(8,128)S(1)} copy-done((f32[64,688]{1,0:T(8,128)S(1)}, f32[64,688]{1,0:T(8,128)}, u32[]{:S(2)}) %copy-start.1) | copy-done | bytes 176152
  3.1 68.5 %shard_map.85 = (bf16[688,512]{1,0:T(8,128)(2,1)S(1)}, f32[64,688]{1,0:T(8,128)S(1)}, f32[64,688]{1,0:T(8,128)S(1)}) custom-call(bf16[512,4096]{1,0:T(8,128)(2,1)} %act_hbm.1, bf16[688,8192]{1,0:T(8,128)(2,1)} %bitcast.2, bf16[4096,512]{1,0:T(8,128)(2,1)} %proj_hbm.1, f32[64,688]{1,0:T(8,128)S(1)} %copy-done, f32[64,688]{1,0:T(8,128)S(1)} %copy-done.1, ...), custom_call_target="tpu_custom_call" | custom-call | flops 8999999488 | bytes 25000000 | tf_op jit(solution)/shard_map/pallas_call | solution.py:333
  71.6 1.0 %shard_map.86 = (bf16[688,512]{1,0:T(8,128)(2,1)}, f32[64,688]{1,0:T(8,128)}, f32[64,688]{1,0:T(8,128)}) custom-call(bf16[688,512]{1,0:T(8,128)(2,1)S(1)} %get-tuple-element.9.refs_0_, f32[64,688]{1,0:T(8,128)S(1)} %get-tuple-element.10.refs_1_, f32[64,688]{1,0:T(8,128)S(1)} %get-tuple-element.11.refs_2_), custom_call_target="tpu_custom_call" | custom-call | tf_op jit(solution)/shard_map/pallas_call | solution.py:301
Async XLA Ops:
  1.3 0.9 %copy-start = (f32[64,688]{1,0:T(8,128)S(1)}, f32[64,688]{1,0:T(8,128)}, u32[]{:S(2)}) copy-start(f32[64,688]{1,0:T(8,128)} %first_hbm.1) | copy-start | bytes 528388
  2.2 0.9 %copy-start.1 = (f32[64,688]{1,0:T(8,128)S(1)}, f32[64,688]{1,0:T(8,128)}, u32[]{:S(2)}) copy-start(f32[64,688]{1,0:T(8,128)} %second_hbm.1) | copy-start | bytes 528388

commit v3 on v2

--- a/solution.py
+++ b/solution.py
@@ -21,6 +21,10 @@
 SHARES = tuple(c // NDP for c in CHUNKS)
 STARTS = tuple(sum(SHARES[:i]) for i in range(len(CHUNKS)))
 NC = len(CHUNKS)
+PIECES = tuple((c, 0, FC) for c in range(NC - 1)) + ((NC - 1, 0, 384), (NC - 1, 384, FC - 384))
+NP = len(PIECES)
+PIECES_OF = tuple(tuple(p for p in range(NP) if PIECES[p][0] == c) for c in range(NC))
+PART_TYPES = tuple(BF for c, _, _ in PIECES)
 KSTEPS = 4
 KW = D // KSTEPS
 GROUP = 4 * HALF
@@ -39,15 +43,15 @@
 
 
 def kernel(
-    act_hbm, cot_hbm, proj_hbm, first_hbm, second_hbm, step_hbm,
+    act_hbm, cot_hbm, proj_hbm, step_hbm, state,
     upd_out, nfirst, nsecond,
-    step_now, act, proj, cot, first, second, eye, projt, upd_acc,
+    step_now, act, proj, cot, eye, projt, upd_acc,
     *rest,
 ):
     gath, acc = rest[:NC], rest[NC : 2 * NC]
-    part, parts_in = rest[2 * NC : 3 * NC], rest[3 * NC : 4 * NC]
-    steps = rest[4 * NC : 5 * NC]
-    load_sem, cot_sem, ssem, rsem, part_ssem, part_rsem, step_ssem, step_rsem = rest[5 * NC :]
+    rest = rest[2 * NC :]
+    part, parts_in, steps = rest[:NP], rest[NP : 2 * NP], rest[2 * NP : 3 * NP]
+    load_sem, cot_sem, ssem, rsem, part_ssem, part_rsem, step_ssem, step_rsem = rest[3 * NP :]
 
     d = lax.axis_index("dp")
     t = lax.axis_index("tensor")
@@ -64,13 +68,15 @@
 
     loads = []
     for k in range(KSTEPS):
-        loads.append(pltpu.make_async_copy(act_hbm.at[:, pl.ds(k * KW, KW)], act.at[:, pl.ds(k * KW, KW)], load_sem.at[2 * k]))
+        part_k = (pl.ds(0, HALF), pl.ds(k * KW, KW))
+        loads.append(pltpu.make_async_copy(act_hbm.at[part_k], act.at[part_k], load_sem.at[2 * k]))
         loads.append(pltpu.make_async_copy(proj_hbm.at[pl.ds(k * KW, KW)], proj.at[pl.ds(k * KW, KW)], load_sem.at[2 * k + 1]))
-    loads.append(pltpu.make_async_copy(first_hbm, first, load_sem.at[2 * KSTEPS]))
-    loads.append(pltpu.make_async_copy(second_hbm, second, load_sem.at[2 * KSTEPS + 1]))
+    late = pl.ds(HALF, HALF)
+    late_load = pltpu.make_async_copy(act_hbm.at[late], act.at[late], load_sem.at[2 * KSTEPS + 3])
     loads.append(pltpu.make_async_copy(step_hbm, step_now, load_sem.at[2 * KSTEPS + 2]))
     for c in loads[: 2 * KSTEPS]:
         c.start()
+    late_load.start()
 
     barrier = pltpu.get_barrier_semaphore()
     for axis in (0, 1):
@@ -149,57 +155,67 @@
         else:
             acc[c][...] += value
 
-    def part_copy(c, j):
+    def part_copy(p, j):
         return pltpu.make_async_remote_copy(
-            part[c].at[(d + j) % NDP], parts_in[c].at[j - 1], part_ssem.at[c], part_rsem.at[c],
+            part[p].at[(d + j) % NDP], parts_in[p].at[j - 1], part_ssem.at[p], part_rsem.at[p],
             device_id=peer(j), device_id_type=MESH,
         )
 
-    def step_copy(c, j):
+    def step_copy(p, j):
         return pltpu.make_async_remote_copy(
-            steps[c].at[d], steps[c].at[d], step_ssem.at[c], step_rsem.at[c],
+            steps[p].at[d], steps[p].at[d], step_ssem.at[p], step_rsem.at[p],
             device_id=peer(j), device_id_type=MESH,
         )
 
-    def share_parts(c):
+    def seven(ref, sem):
+        ref = ref.at[pl.ds(0, NDP - 1)]
+        pltpu.make_async_copy(ref, ref, sem).wait()
+
+    def share_parts(p):
+        c, start, width = PIECES[p]
+        own = acc[c][:, start : start + width]
+        part[p][...] = own.reshape(NDP, SHARES[c], width).astype(PART_TYPES[p])
+        for j in range(1, NDP):
+            part_copy(p, j).start()
+
+    def adam(p):
+        c, start, width = PIECES[p]
         share = SHARES[c]
-        part[c][...] = acc[c][...].reshape(NDP, share, FC).astype(BF)
-        for j in range(1, NDP):
-            part_copy(c, j).start()
-
-    def adam(c):
-        share, start = SHARES[c], STARTS[c]
-        t_value = jnp.full((8, 128), step_now[0].astype(F32), F32)
+        cols = slice(start, start + width)
+        t_value = step_now[...].astype(F32)
         fix_first = (1.0 / (1.0 - jnp.power(jnp.full((8, 128), 0.9, F32), t_value)))[0:1, 0:1]
         fix_second = (1.0 / (1.0 - jnp.power(jnp.full((8, 128), 0.999, F32), t_value)))[0:1, 0:1]
-        grad = acc[c][pl.ds(pl.multiple_of(d * share, share), share), :]
-        pltpu.make_async_copy(parts_in[c], parts_in[c], part_rsem.at[c]).wait()
+        grad = acc[c][pl.ds(pl.multiple_of(d * share, share), share), cols]
+        seven(parts_in[p], part_rsem.at[p])
         for j in range(1, NDP):
-            grad = grad + parts_in[c][j - 1].astype(F32)
-        rows = pl.ds(start, share)
-        new_first = 0.9 * first[rows, :] + 0.1 * grad
-        new_second = 0.999 * second[rows, :] + 0.001 * grad * grad
-        nfirst[rows, :] = new_first
-        nsecond[rows, :] = new_second
+            grad = grad + parts_in[p][j - 1].astype(F32)
+        rows = slice(STARTS[c], STARTS[c] + share)
+        new_first = 0.9 * state[rows, cols] + 0.1 * grad
+        new_second = 0.999 * state[PER + STARTS[c] : PER + STARTS[c] + share, cols] + 0.001 * grad * grad
+        nfirst[rows, cols] = new_first
+        nsecond[rows, cols] = new_second
         normalized = (new_first * fix_first) / (jnp.sqrt(new_second * fix_second) + 1e-08)
-        steps[c][d] = normalized.astype(BF)
+        steps[p][d] = normalized.astype(BF)
         for j in range(1, NDP):
-            step_copy(c, j).start()
-
-    def update(c):
-        seven = steps[c].at[pl.ds(0, NDP - 1)]
-        pltpu.make_async_copy(seven, seven, step_rsem.at[c]).wait()
-        chunk = steps[c][...].astype(F32).reshape(CHUNKS[c], FC)
+            step_copy(p, j).start()
+
+    def update(p):
+        c, start, width = PIECES[p]
+        seven(steps[p], step_rsem.at[p])
+        chunk = steps[p][...].astype(F32).reshape(CHUNKS[c], width)
         value = dot(chunk.T.astype(BF), projt[pl.ds(sum(CHUNKS[:c]), CHUNKS[c]), :], 1, 0)
         if c == 0:
             upd_acc[...] = value
         elif c < NC - 1:
             upd_acc[...] += value
         else:
-            upd_out[...] = (upd_acc[...] + value).astype(BF)
+            rows = slice(start, start + width)
+            upd_out[rows, :] = (upd_acc[rows, :] + value).astype(BF)
 
     for h in (0, 1):
         total = None
+        if h == 1:
+            late_load.wait()
         for k in range(KSTEPS):
             if h == 0:
                 loads[2 * k].wait()
@@ -269,22 +285,25 @@
     for h in (0, 1):
         far_second(NC - 1, h)
         add_group(NC - 1, h, 2)
-    share_parts(NC - 1)
+    for p in PIECES_OF[NC - 1]:
+        share_parts(p)
     adam(NC - 2)
     update(NC - 3)
     for c in range(NC):
         sent(c)
-    for c in range(NC - 1):
-        pltpu.make_async_copy(parts_in[c], parts_in[c], part_ssem.at[c]).wait()
-    adam(NC - 1)
-    for c in range(NC - 1):
-        seven = steps[c].at[pl.ds(0, NDP - 1)]
-        pltpu.make_async_copy(seven, seven, step_ssem.at[c]).wait()
+    for p in range(NC - 1):
+        seven(parts_in[p], part_ssem.at[p])
+    for p in PIECES_OF[NC - 1]:
+        adam(p)
+    for p in range(NC - 2):
+        seven(steps[p], step_ssem.at[p])
     update(NC - 2)
-    update(NC - 1)
-    pltpu.make_async_copy(parts_in[NC - 1], parts_in[NC - 1], part_ssem.at[NC - 1]).wait()
-    seven = steps[NC - 1].at[pl.ds(0, NDP - 1)]
-    pltpu.make_async_copy(seven, seven, step_ssem.at[NC - 1]).wait()
+    for p in PIECES_OF[NC - 1]:
+        update(p)
+    for p in PIECES_OF[NC - 1]:
+        seven(parts_in[p], part_ssem.at[p])
+    for p in range(NC - 2, NP):
+        seven(steps[p], step_ssem.at[p])
 
 
 def write_out(*arrays):
@@ -310,25 +329,23 @@
 
 def per_device(activations, cotangent, projection, first_moment, second_moment, step_count):
     scratch = [
-        pltpu.SMEM((1,), jnp.int32),
+        pltpu.VMEM((8, 128), jnp.int32),
         pltpu.VMEM((TOK, D), BF),
         pltpu.VMEM((D, R), BF),
         pltpu.VMEM((2, NT, FC, HALF), BF),
-        pltpu.VMEM((PER, FC), F32),
-        pltpu.VMEM((PER, FC), F32),
         pltpu.VMEM((R, R), BF),
         pltpu.VMEM((R, DR), BF),
         pltpu.VMEM((FC, DR), F32),
     ]
     scratch += [pltpu.VMEM((2, NT, c, HALF), BF) for c in CHUNKS]
     scratch += [pltpu.VMEM((c, FC), F32) for c in CHUNKS]
-    scratch += [pltpu.VMEM((NDP, s, FC), BF) for s in SHARES]
-    scratch += [pltpu.VMEM((NDP - 1, s, FC), BF) for s in SHARES]
-    scratch += [pltpu.VMEM((NDP, s, FC), BF) for s in SHARES]
+    scratch += [pltpu.VMEM((NDP, SHARES[c], w), ty) for (c, _, w), ty in zip(PIECES, PART_TYPES)]
+    scratch += [pltpu.VMEM((NDP - 1, SHARES[c], w), ty) for (c, _, w), ty in zip(PIECES, PART_TYPES)]
+    scratch += [pltpu.VMEM((NDP, SHARES[c], w), BF) for c, _, w in PIECES]
     dma = pltpu.SemaphoreType.DMA
     scratch += [
-        dma((2 * KSTEPS + 3,)), dma((1,)), dma((NC, 2)), dma((NC, 2, 7)),
-        dma((NC,)), dma((NC,)), dma((NC,)), dma((NC,)),
+        dma((2 * KSTEPS + 4,)), dma((1,)), dma((NC, 2)), dma((NC, 2, 7)),
+        dma((NP,)), dma((NP,)), dma((NP,)), dma((NP,)),
     ]
     update_t, new_first, new_second = pl.pallas_call(
         kernel,
@@ -337,14 +354,14 @@
             jax.ShapeDtypeStruct((PER, FC), F32),
             jax.ShapeDtypeStruct((PER, FC), F32),
         ),
-        in_specs=[pl.BlockSpec(memory_space=pltpu.HBM)] * 6,
+        in_specs=[pl.BlockSpec(memory_space=pltpu.HBM)] * 4 + [pl.BlockSpec(memory_space=pltpu.VMEM)],
         out_specs=[pl.BlockSpec(memory_space=pltpu.VMEM)] * 3,
         scratch_shapes=scratch,
         compiler_params=pltpu.CompilerParams(
             collective_id=0, has_side_effects=True, vmem_limit_bytes=int(VMEM_MIB * 2**20)
         ),
         cost_estimate=pl.CostEstimate(flops=9 * 10**9, bytes_accessed=25 * 10**6, transcendentals=0),
-    )(activations, cotangent.T, projection, first_moment, second_moment, step_count)
+    )(activations, cotangent.T, projection, jnp.pad(step_count.reshape(1, 1), ((0, 7), (0, 127))), jnp.concatenate([first_moment, second_moment], axis=0))
     update_t, new_first, new_second = write_out(update_t, new_first, new_second)
     return update_t.T, new_first, new_second
 

time: 72.8 us -> 71 us (0.975)
  local copies, waits for them, and re-layouts: 1.85 us -> 0.01 us
  other arithmetic: 0 us -> 1.05 us
  Pallas kernels: 69.5 us -> 68.5 us
    unnamed x4 -> x0, local copies, waits for them, and re-layouts: 1.85 us -> none
    concatenate x0 -> x1, other arithmetic: none -> 1.05 us  [per_device(): jnp.concatenate([first_moment, second_moment], axis=0)]
    pallas_call x1, Pallas kernels: 68.5 us -> 67.5 us  [per_device(): pl.pallas_call(kernel, out_shape=(jax.ShapeDtypeStruct((FC, DR), BF), jax...]
where the time goes in v3:
time: 71 us; the launch traced here: 70.8 us
  Pallas kernels  68.5 us (96%)
  between operations  1.29 us (2%)
  other arithmetic  1.05 us (1%)
    pallas_call x1, Pallas kernels, per_device(): pl.pallas_call(kernel, out_shape=(jax.ShapeDtypeStruct((FC, DR), BF), jax...  67.5 us

profile of v3, /device:TPU:1, one launch (start us, length us, event | category | flops | bytes accessed | tf_op | source)
XLA Modules:
  0.0 70.8 jit_solution(5188324057578431755)
XLA Ops:
  1.3 1.1 %pad_maximum_fusion.state = f32[128,688]{1,0:T(8,128)S(1)} fusion(f32[64,688]{1,0:T(8,128)} %param.10, f32[64,688]{1,0:T(8,128)} %param.9), kind=kLoop, calls=%fused_computation | loop fusion | flops 88064 | bytes 704512 | tf_op jit(solution)/shard_map/concatenate | solution.py:364
  2.3 67.5 %shard_map.85 = (bf16[688,512]{1,0:T(8,128)(2,1)S(1)}, f32[64,688]{1,0:T(8,128)S(1)}, f32[64,688]{1,0:T(8,128)S(1)}) custom-call(bf16[512,4096]{1,0:T(8,128)(2,1)} %act_hbm.1, bf16[688,8192]{1,0:T(8,128)(2,1)} %bitcast.4, bf16[4096,512]{1,0:T(8,128)(2,1)} %proj_hbm.1, s32[8,128]{1,0:T(8,128)S(1)} %pad.4.step_hbm, f32[128,688]{1,0:T(8,128)S(1)} %pad_maximum_fusion.state), custom_call_target="tpu_custom_call" | custom-call | flops 8999999488 | bytes 25000000 | tf_op jit(solution)/shard_map/pallas_call | solution.py:350
  69.8 1.0 %shard_map.86 = (bf16[688,512]{1,0:T(8,128)(2,1)}, f32[64,688]{1,0:T(8,128)}, f32[64,688]{1,0:T(8,128)}) custom-call(bf16[688,512]{1,0:T(8,128)(2,1)S(1)} %get-tuple-element.9.refs_0_, f32[64,688]{1,0:T(8,128)S(1)} %get-tuple-element.10.refs_1_, f32[64,688]{1,0:T(8,128)S(1)} %get-tuple-element.11.refs_2_), custom_call_target="tpu_custom_call" | custom-call | tf_op jit(solution)/shard_map/pallas_call | solution.py:320
  (1 shorter events, 0.0 us)

commit v4 on v3

--- a/solution.py
+++ b/solution.py
@@ -30,6 +30,7 @@
 GROUP = 4 * HALF
 VMEM_MIB = 52
 OFFSETS = (0, -1, 1, 2)
+FAR_FIRST = (4, 3, 5, 2, 6, 1, 7)
 
 
 def dot(a, b, ca, cb):
@@ -175,7 +176,7 @@
         c, start, width = PIECES[p]
         own = acc[c][:, start : start + width]
         part[p][...] = own.reshape(NDP, SHARES[c], width).astype(PART_TYPES[p])
-        for j in range(1, NDP):
+        for j in FAR_FIRST:
             part_copy(p, j).start()
 
     def adam(p):
@@ -196,7 +197,7 @@
         nsecond[rows, cols] = new_second
         normalized = (new_first * fix_first) / (jnp.sqrt(new_second * fix_second) + 1e-08)
         steps[p][d] = normalized.astype(BF)
-        for j in range(1, NDP):
+        for j in FAR_FIRST:
             step_copy(p, j).start()
 
     def update(p):
@@ -234,8 +235,7 @@
                 c.start()
         own_first(0, h)
         to_second(0, h, 0)
-    for c in range(1, NC):
-        for h in (0, 1):
+        for c in range(1, NC):
             own_first(c, h)
     turned = dot(eye[...], proj[pl.ds(pl.multiple_of(d * DR, DR), DR), :], 1, 1)
     for c in range(NC):

time: 71 us -> 70.1 us (0.987)
  Pallas kernels: 68.5 us -> 67.6 us
    pallas_call x1, Pallas kernels: 67.5 us -> 66.6 us  [per_device(): pl.pallas_call(kernel, out_shape=(jax.ShapeDtypeStruct((FC, DR), BF), jax...]
where the time goes in v4:
time: 70.1 us; the launch traced here: 70 us
  Pallas kernels  67.6 us (96%)
  between operations  1.29 us (2%)
  other arithmetic  1.05 us (1%)
    pallas_call x1, Pallas kernels, per_device(): pl.pallas_call(kernel, out_shape=(jax.ShapeDtypeStruct((FC, DR), BF), jax...  66.6 us

profile of v4, /device:TPU:1, one launch (start us, length us, event | category | flops | bytes accessed | tf_op | source)
XLA Modules:
  0.0 70.0 jit_solution(7528666797098232333)
XLA Ops:
  1.3 1.1 %pad_maximum_fusion.state = f32[128,688]{1,0:T(8,128)S(1)} fusion(f32[64,688]{1,0:T(8,128)} %param.10, f32[64,688]{1,0:T(8,128)} %param.9), kind=kLoop, calls=%fused_computation | loop fusion | flops 88064 | bytes 704512 | tf_op jit(solution)/shard_map/concatenate | solution.py:364
  2.3 66.6 %shard_map.85 = (bf16[688,512]{1,0:T(8,128)(2,1)S(1)}, f32[64,688]{1,0:T(8,128)S(1)}, f32[64,688]{1,0:T(8,128)S(1)}) custom-call(bf16[512,4096]{1,0:T(8,128)(2,1)} %act_hbm.1, bf16[688,8192]{1,0:T(8,128)(2,1)} %bitcast.4, bf16[4096,512]{1,0:T(8,128)(2,1)} %proj_hbm.1, s32[8,128]{1,0:T(8,128)S(1)} %pad.4.step_hbm, f32[128,688]{1,0:T(8,128)S(1)} %pad_maximum_fusion.state), custom_call_target="tpu_custom_call" | custom-call | flops 8999999488 | bytes 25000000 | tf_op jit(solution)/shard_map/pallas_call | solution.py:350
  69.0 1.0 %shard_map.86 = (bf16[688,512]{1,0:T(8,128)(2,1)}, f32[64,688]{1,0:T(8,128)}, f32[64,688]{1,0:T(8,128)}) custom-call(bf16[688,512]{1,0:T(8,128)(2,1)S(1)} %get-tuple-element.9.refs_0_, f32[64,688]{1,0:T(8,128)S(1)} %get-tuple-element.10.refs_1_, f32[64,688]{1,0:T(8,128)S(1)} %get-tuple-element.11.refs_2_), custom_call_target="tpu_custom_call" | custom-call | tf_op jit(solution)/shard_map/pallas_call | solution.py:320
  (1 shorter events, 0.0 us)

commit v5 on v4

--- a/solution.py
+++ b/solution.py
@@ -21,7 +21,7 @@
 SHARES = tuple(c // NDP for c in CHUNKS)
 STARTS = tuple(sum(SHARES[:i]) for i in range(len(CHUNKS)))
 NC = len(CHUNKS)
-PIECES = tuple((c, 0, FC) for c in range(NC - 1)) + ((NC - 1, 0, 384), (NC - 1, 384, FC - 384))
+PIECES = tuple((c, 0, FC) for c in range(NC - 1)) + ((NC - 1, 0, 256), (NC - 1, 256, FC - 256))
 NP = len(PIECES)
 PIECES_OF = tuple(tuple(p for p in range(NP) if PIECES[p][0] == c) for c in range(NC))
 PART_TYPES = tuple(BF for c, _, _ in PIECES)
@@ -146,15 +146,15 @@
             ref = gath[c].at[h, pl.ds(0, 15)]
             pltpu.make_async_copy(ref, ref, ssem.at[c, h]).wait()
 
-    def add_group(c, h, v, fresh=False):
+    def add_group(c, h, v, fresh=False, cols=slice(0, FC)):
         at = ((pos[h][1] + v + 4) % 4) * 4
         p = jnp.concatenate([gath[c][h, at + u] for u in range(4)], axis=1)
-        g = jnp.concatenate([cot[h, at + u] for u in range(4)], axis=1)
+        g = jnp.concatenate([cot[h, at + u, cols, :] for u in range(4)], axis=1)
         value = dot(p, g, 1, 1)
         if fresh:
             acc[c][...] = value
         else:
-            acc[c][...] += value
+            acc[c][:, cols] += value
 
     def part_copy(p, j):
         return pltpu.make_async_remote_copy(
@@ -229,14 +229,15 @@
             gath[c][h, place(h, 0, 0)] = jnp.concatenate(rows, axis=0).astype(BF)
         if h == 0:
             pl.semaphore_wait(barrier, 4 + NDP - 1)
+        own_first(0, h)
+        to_second(0, h, 0)
+        for c in range(1, NC):
+            own_first(c, h)
+        if h == 0:
             for c in loads[2 * KSTEPS :]:
                 c.start()
             for c in cot_loads.values():
                 c.start()
-        own_first(0, h)
-        to_second(0, h, 0)
-        for c in range(1, NC):
-            own_first(c, h)
     turned = dot(eye[...], proj[pl.ds(pl.multiple_of(d * DR, DR), DR), :], 1, 1)
     for c in range(NC):
         rows = [turned[PER * e + STARTS[c] : PER * e + STARTS[c] + SHARES[c]] for e in range(NDP)]
@@ -282,10 +283,11 @@
             share_parts(i - 1)
         add_group(i, 1, -1)
         add_group(i, 1, 1)
-    for h in (0, 1):
-        far_second(NC - 1, h)
-        add_group(NC - 1, h, 2)
+    far_second(NC - 1, 0)
+    add_group(NC - 1, 0, 2)
+    far_second(NC - 1, 1)
     for p in PIECES_OF[NC - 1]:
+        add_group(NC - 1, 1, 2, cols=slice(PIECES[p][1], PIECES[p][1] + PIECES[p][2]))
         share_parts(p)
     adam(NC - 2)
     update(NC - 3)

time: 70.1 us -> 69.9 us (level)
  no operation moved by 1% of the time
where the time goes in v5:
time: 69.9 us; the launch traced here: 69.8 us
  Pallas kernels  67.4 us (96%)
  between operations  1.29 us (2%)
  other arithmetic  1.05 us (2%)
    pallas_call x1, Pallas kernels, per_device(): pl.pallas_call(kernel, out_shape=(jax.ShapeDtypeStruct((FC, DR), BF), jax...  66.4 us

profile of v5, /device:TPU:1, one launch (start us, length us, event | category | flops | bytes accessed | tf_op | source)
XLA Modules:
  0.0 69.8 jit_solution(8269825449914749691)
XLA Ops:
  1.3 1.1 %pad_maximum_fusion.state = f32[128,688]{1,0:T(8,128)S(1)} fusion(f32[64,688]{1,0:T(8,128)} %param.10, f32[64,688]{1,0:T(8,128)} %param.9), kind=kLoop, calls=%fused_computation | loop fusion | flops 88064 | bytes 704512 | tf_op jit(solution)/shard_map/concatenate | solution.py:366
  2.3 66.4 %shard_map.85 = (bf16[688,512]{1,0:T(8,128)(2,1)S(1)}, f32[64,688]{1,0:T(8,128)S(1)}, f32[64,688]{1,0:T(8,128)S(1)}) custom-call(bf16[512,4096]{1,0:T(8,128)(2,1)} %act_hbm.1, bf16[688,8192]{1,0:T(8,128)(2,1)} %bitcast.4, bf16[4096,512]{1,0:T(8,128)(2,1)} %proj_hbm.1, s32[8,128]{1,0:T(8,128)S(1)} %pad.4.step_hbm, f32[128,688]{1,0:T(8,128)S(1)} %pad_maximum_fusion.state), custom_call_target="tpu_custom_call" | custom-call | flops 8999999488 | bytes 25000000 | tf_op jit(solution)/shard_map/pallas_call | solution.py:352
  68.8 1.0 %shard_map.86 = (bf16[688,512]{1,0:T(8,128)(2,1)}, f32[64,688]{1,0:T(8,128)}, f32[64,688]{1,0:T(8,128)}) custom-call(bf16[688,512]{1,0:T(8,128)(2,1)S(1)} %get-tuple-element.9.refs_0_, f32[64,688]{1,0:T(8,128)S(1)} %get-tuple-element.10.refs_1_, f32[64,688]{1,0:T(8,128)S(1)} %get-tuple-element.11.refs_2_), custom_call_target="tpu_custom_call" | custom-call | tf_op jit(solution)/shard_map/pallas_call | solution.py:322
  (1 shorter events, 0.0 us)
